TPU v7x, 512 devices: a whole 4x4x16 slice. The times are simulated.
512 devices in a mesh: row: 8 (over y, z_hi), col: 8 (over x, core), depth: 8 (over z_lo).
Axes of the slice: x: 4, y: 4, z: 16 (z_hi: 2, z_lo: 8; z = z_hi * 8 + z_lo), core: 2. Of those that a mesh axis runs over, the one named last changes fastest.
Arguments:
- tokens: bfloat16 [512, 12288], P('col', 'row'), may hold values from -6 to 6
- weight_in: bfloat16 [12288, 49152], P('row', ('col', 'depth')), may hold values from -0.0546875 to 0.0546875
- bias_in: float32 [49152], P(('col', 'depth')), may hold values from -3 to 3
- weight_out: bfloat16 [49152, 12288], P(('col', 'depth'), 'row'), may hold values from -0.02734375 to 0.02734375
- bias_out: float32 [12288], P('row'), may hold values from -3 to 3
Outputs:
- layer_out: bfloat16 [512, 12288], P(('col', 'depth'), 'row')
All inputs are finite; a program needn't handle non-finite values.
Results may differ from a plain program's by a relative error of at most 0.0045.
Values may be sent and summed in bfloat16 or wider, within the bound.
A program may use at most 64 MiB of HBM per device.

v0:
```python
import jax
import jax.numpy as jnp
from jax import lax
from jax.sharding import PartitionSpec as P


def on_device(tokens, weight_in, bias_in, weight_out, bias_out):
    gathered = lax.all_gather(tokens, "col", axis=0, tiled=True)
    partial_pre = jnp.dot(gathered, weight_in, preferred_element_type=jnp.float32)
    summed_pre = lax.psum(partial_pre, "row")
    hidden_all = jax.nn.gelu(summed_pre + bias_in, approximate=True).astype(jnp.bfloat16)
    summed_out = lax.psum_scatter(
        jnp.dot(hidden_all, weight_out, preferred_element_type=jnp.float32),
        ("col", "depth"),
        scatter_dimension=0,
        tiled=True,
    )
    return (summed_out + bias_out).astype(jnp.bfloat16)


def solution(mesh):
    placed = (
        P("col", "row"),
        P("row", ("col", "depth")),
        P(("col", "depth")),
        P(("col", "depth"), "row"),
        P("row"),
    )
    return jax.shard_map(
        on_device, mesh=mesh, in_specs=placed, out_specs=P(("col", "depth"), "row"), check_vma=False
    )
```

profile of v0, /device:TPU:16, one launch (start us, length us, event | category | flops | bytes accessed | tf_op | source)
XLA Modules:
  0.0 810.8 jit_solution(4857658228943338122)
XLA Ops:
  6.5 0.0 copy-start
  6.5 0.0 all-gather.2.cloned.1.call-start
  6.5 0.7 all-gather.2.cloned.1.call-update
  7.3 0.0 all-reduce.2.cloned.1.call-start
  7.3 38.6 %all-gather.2.cloned.1.call-done = bf16[512,1536]{1,0:T(8,128)(2,1)} async-done(((bf16[64,1536]{1,0:T(8,128)(2,1)}), bf16[512,1536]{1,0:T(8,128)(2,1)}) %all-gather.2.cloned.1.call-update) | async-done | bytes 1572880 | tf_op jit(solution)/shard_map/all_gather | solution.py:8
  45.9 4.7 fusion.19
  50.6 0.0 copy-start.2
  50.6 0.0 all-reduce.2.cloned.1.call-update
  50.7 0.0 reduce-scatter.2.cloned.1.call-start
  50.7 299.9 %all-reduce.2.cloned.1.call-done = f32[512,768]{1,0:T(8,128)} async-done(((f32[512,768]{1,0:T(8,128)}), f32[512,768]{1,0:T(8,128)}) %all-reduce.2.cloned.1.call-update) | async-done | bytes 1572880 | tf_op jit(solution)/shard_map/psum | solution.py:10
  350.6 0.0 copy-done
  350.6 0.0 copy-done.2
  350.6 4.6 fusion.8
  355.2 0.0 copy-start.1
  355.2 0.0 reduce-scatter.2.cloned.1.call-update
  355.2 447.6 %reduce-scatter.2.cloned.1.call-done = f32[8,1536]{1,0:T(8,128)} async-done(((f32[512,1536]{1,0:T(8,128)}), f32[8,1536]{1,0:T(8,128)}) %reduce-scatter.2.cloned.1.call-update) | async-done | bytes 49168 | tf_op jit(solution)/shard_map/reduce_scatter | solution.py:12
  802.8 0.0 copy-done.1
  802.8 1.4 add_convert_fusion
Async XLA Ops:
  6.5 344.1 %copy-start = (bf16[768,1536]{1,0:T(8,128)(2,1)S(1)}, bf16[768,1536]{1,0:T(8,128)(2,1)}, u32[]{:S(2)}) copy-start(bf16[768,1536]{1,0:T(8,128)(2,1)} %param.8) | copy-start | bytes 7077892
  6.5 39.4 %all-gather.2.cloned.1.call-start = ((), (), s32[]{:S(2)}) async-start(), calls=%async_computation.1 | async-start | bytes 1769472 | tf_op jit(solution)/shard_map/all_gather | solution.py:8
  7.3 343.3 %all-reduce.2.cloned.1.call-start = ((), (), s32[]{:S(2)}) async-start(), calls=%async_computation.2 | async-start | bytes 3145728 | tf_op jit(solution)/shard_map/psum | solution.py:10
  50.6 300.0 %copy-start.2 = (f32[768]{0:T(1024)S(1)}, f32[768]{0:T(1024)}, u32[]{:S(2)}) copy-start(f32[768]{0:T(1024)} %param.7) | copy-start | bytes 9220
  50.7 752.2 %reduce-scatter.2.cloned.1.call-start = ((), (), s32[]{:S(2)}) async-start(), calls=%async_computation.3 | async-start | bytes 3194880 | tf_op jit(solution)/shard_map/reduce_scatter | solution.py:12
  355.2 447.6 %copy-start.1 = (f32[1536]{0:T(1024)S(1)}, f32[1536]{0:T(1024)}, u32[]{:S(2)}) copy-start(f32[1536]{0:T(1024)} %param.9) | copy-start | bytes 18436
Sparse Core Ops, SparseCore 0:
  9.5 36.4 all-gather.1
  50.8 299.7 all-reduce.1
  355.3 447.4 reduce-scatter.1
where the time goes:
time: 811 us
  waiting for transfers between devices  787 us (97%)
  between operations  13.1 us (2%)
  matrix products  9.27 us (1%)
    reduce_scatter x1, waiting for transfers between devices, on_device(): lax.psum_scatter(jnp.dot(hidden_all, weight_out, preferred_element_type=j...  448 us
    psum x1, waiting for transfers between devices, on_device(): summed_pre = lax.psum(partial_pre, 'row')  300 us
    all_gather x1, waiting for transfers between devices, on_device(): gathered = lax.all_gather(tokens, 'col', axis=0, tiled=True)  38.6 us
  transfers between devices with their start and end apart: 3, of which 3 were waited for; matrix products, arithmetic and copies ran while one was open for 0% of the time, Pallas kernels for 0%

commit v1 on v0

v1 whole, which is shorter than its diff:
```python
import jax
import jax.numpy as jnp
from jax import lax
from jax.experimental import pallas as pl
from jax.experimental.pallas import tpu as pltpu
from jax.sharding import PartitionSpec as P

CHUNKS = 4
TOKENS, WIDTH, UNITS = 512, 1536, 768
CHUNK = TOKENS // CHUNKS
MINE = CHUNK // 8
PIECE = CHUNK // 4
DEPTHS = MINE // 8
TILE = 256
HALF = WIDTH // 2


def remote(src, dst, send, recv, device):
    return pltpu.make_async_remote_copy(
        src_ref=src,
        dst_ref=dst,
        send_sem=send,
        recv_sem=recv,
        device_id=device,
        device_id_type=pl.DeviceIdType.MESH,
    )


def kernel(
    tokens, weight_in, bias_in, weight_out, bias_out, out,
    w_in, w_out, gathered, pre_send, pre_recv, pre_sum, pre_out, pre_other, hidden,
    total, total_other, x_send, x_recv, x_sum, z_send, z_recv,
    local_sem, tok_ss, tok_rs, sib_ss, sib_rs, pre_ss, pre_rs, half_ss, half_rs,
    hid_ss, hid_rs, core_ss, core_rs, x_ss, x_rs, z_ss, z_rs,
):
    row, col, depth = lax.axis_index("row"), lax.axis_index("col"), lax.axis_index("depth")
    y, z_hi, x, core = row // 2, row % 2, col // 2, col % 2

    def at_x(step):
        return {"col": ((x + step) % 4) * 2 + core}

    def at_y(step):
        return {"row": ((y + step) % 4) * 2 + z_hi}

    sibling = {"col": x * 2 + 1 - core}
    other_half = {"row": y * 2 + 1 - z_hi}

    def at_depth(d):
        return {"depth": d}

    own = pl.ds(pl.multiple_of(col * MINE, MINE), MINE)
    get_w_in = pltpu.make_async_copy(weight_in, w_in, local_sem.at[CHUNKS])
    get_w_out = pltpu.make_async_copy(weight_out, w_out, local_sem.at[CHUNKS + 1])
    get_own = [
        pltpu.make_async_copy(
            tokens.at[pl.ds(k * MINE, MINE)], gathered.at[k, own], local_sem.at[k]
        )
        for k in range(CHUNKS)
    ]
    for copy in get_own:
        copy.start()
    get_w_in.start()
    get_w_out.start()

    barrier = pltpu.get_barrier_semaphore()
    partners = [at_x(1), at_x(2), at_x(3), at_y(1), at_y(2), at_y(3), sibling, other_half]
    partners += [at_depth((depth + s) % 8) for s in range(1, 8)]
    for device in partners:
        pl.semaphore_signal(barrier, inc=1, device_id=device, device_id_type=pl.DeviceIdType.MESH)
    pl.semaphore_wait(barrier, len(partners))

    def tok_copy(k, s):
        return remote(
            tokens.at[pl.ds(k * MINE, MINE)], gathered.at[k, own],
            tok_ss.at[k, s - 1], tok_rs.at[k, s - 1], at_x(s),
        )

    def tok_place(step, which):
        c = ((x + 4 - step) % 4) * 2 + which
        return pl.ds(pl.multiple_of(c * MINE, MINE), MINE)

    def sib_copy(k, s, which):
        place = tok_place(s, which)
        src = tokens.at[pl.ds(k * MINE, MINE)] if s == 0 else gathered.at[k, place]
        return remote(src, gathered.at[k, place], sib_ss.at[k, s], sib_rs.at[k, s], sibling)

    def pre_copy(k, s):
        piece = pl.ds(pl.multiple_of(((y + s) % 4) * PIECE, PIECE), PIECE)
        return remote(
            pre_send.at[k, piece], pre_recv.at[k, s - 1],
            pre_ss.at[k, s - 1], pre_rs.at[k, s - 1], at_y(s),
        )

    def half_copy(k):
        return remote(pre_out.at[k], pre_other.at[k], half_ss.at[k], half_rs.at[k], other_half)

    my_piece = pl.ds(pl.multiple_of(y * PIECE, PIECE), PIECE)

    def hid_copy(k, s):
        return remote(
            hidden.at[k, my_piece], hidden.at[k, my_piece],
            hid_ss.at[k, s - 1], hid_rs.at[k, s - 1], at_y(s),
        )

    def core_copy(k, i):
        rows = pl.ds(pl.multiple_of((2 * i + 1 - core) * MINE, MINE), MINE)
        return remote(
            total.at[k, rows], total_other.at[k, i], core_ss.at[k, i], core_rs.at[k, i], sibling
        )

    def x_copy(k, s):
        return remote(
            x_send.at[k, s - 1], x_recv.at[k, s - 1], x_ss.at[k, s - 1], x_rs.at[k, s - 1], at_x(s)
        )

    def z_copy(d, to):
        return remote(z_send.at[d], z_recv.at[depth], z_ss.at[d], z_rs.at[depth], at_depth(to))

    def forward(k):
        for s in range(1, 4):
            tok_copy(k, s).wait_recv()
            sib_copy(k, s, core).start()

    def first_product(k):
        get_own[k].wait()
        for s in range(4):
            sib_copy(k, s, 1 - core).wait_recv()
        if k == 0:
            get_w_in.wait()

        def tile(i, _):
            units = pl.ds(pl.multiple_of(i * TILE, TILE), TILE)
            part = jnp.dot(gathered[k], w_in[:, units], preferred_element_type=jnp.float32)
            pre_send[k, :, units] = part.astype(jnp.bfloat16)
            pre_sum[:, units] = part
            return 0

        lax.fori_loop(0, UNITS // TILE, tile, 0)
        for s in range(1, 4):
            pre_copy(k, s).start()
        keep[k] = pre_sum[my_piece, :]

    keep = {}

    def sum_pieces(k):
        acc = keep.pop(k)
        for s in range(1, 4):
            pre_copy(k, s).wait_recv()
            acc = acc + pre_recv[k, s - 1].astype(jnp.float32)
        pre_out[k] = acc.astype(jnp.bfloat16)
        half_copy(k).start()
        keep[k] = acc

    def activate(k):
        half_copy(k).wait_recv()
        v = keep.pop(k) + pre_other[k].astype(jnp.float32) + bias_in[...]
        hidden[k, my_piece, :] = jax.nn.gelu(v, approximate=True).astype(jnp.bfloat16)
        for s in range(1, 4):
            hid_copy(k, s).start()

    def second_product(k):
        for s in range(1, 4):
            hid_copy(k, s).wait_recv()
        if k == 0:
            get_w_out.wait()

        def tile(i, _):
            cols = pl.ds(pl.multiple_of(i * TILE, TILE), TILE)
            total[k, :, cols] = jnp.dot(
                hidden[k], w_out[:, cols], preferred_element_type=jnp.float32
            )
            return 0

        lax.fori_loop(0, WIDTH // TILE, tile, 0)
        for i in range(4):
            core_copy(k, i).start()

    def sum_cores(k):
        for i in range(4):
            core_copy(k, i).wait_recv()
        for s in (1, 2, 3, 0):
            i = (x + s) % 4
            rows = pl.ds(pl.multiple_of((2 * i + core) * MINE, MINE), MINE)
            part = total[k, rows, :] + total_other[k, i]
            if s:
                x_send[k, s - 1] = part.astype(jnp.bfloat16)
                x_copy(k, s).start()
            else:
                x_sum[k] = part

    def sum_x(k):
        acc = x_sum[k]
        for s in range(1, 4):
            x_copy(k, s).wait_recv()
            acc = acc + x_recv[k, s - 1].astype(jnp.float32)
        for n in range(DEPTHS):
            d = k * DEPTHS + n
            part = acc[n * 8:(n + 1) * 8]
            folded = jnp.concatenate([part[:, :HALF], part[:, HALF:]], axis=0)

            @pl.when(depth == d)
            def _():
                out[...] = part

            @pl.when(depth != d)
            def _():
                z_send[d] = folded.astype(jnp.bfloat16)
                z_copy(d, d).start()

    for k in range(CHUNKS):
        for s in (2, 1, 3):
            tok_copy(k, s).start()
        sib_copy(k, 0, core).start()

    stages = (
        (forward, 0.0, 2.0), (first_product, 1.0, 2.0), (sum_pieces, 5.0, 2.0), (activate, 10.0, 4.5),
        (second_product, 13.0, 4.5), (sum_cores, 14.5, 4.5), (sum_x, 17.5, 4.5),
    )
    order = sorted(
        (start + k * gap, n, k) for n, (_, start, gap) in enumerate(stages) for k in range(CHUNKS)
    )
    for _, n, k in order:
        stages[n][0](k)

    acc = out[...] + bias_out[...]
    for s in range(1, 8):
        d = (depth + s) % 8
        remote(z_send.at[d], z_recv.at[d], z_ss.at[d], z_rs.at[d], at_depth(d)).wait_recv()
        part = z_recv[d].astype(jnp.float32)
        acc = acc + jnp.concatenate([part[:8], part[8:]], axis=1)
    out[...] = acc

    for k in range(CHUNKS):
        for s in range(1, 4):
            tok_copy(k, s).wait_send()
            pre_copy(k, s).wait_send()
            hid_copy(k, s).wait_send()
            x_copy(k, s).wait_send()
        for s in range(4):
            sib_copy(k, s, core).wait_send()
            core_copy(k, s).wait_send()
        half_copy(k).wait_send()
    for d in range(8):
        @pl.when(depth != d)
        def _():
            z_copy(d, d).wait_send()


def on_device(tokens, weight_in, bias_in, weight_out, bias_out):
    bf16, f32 = jnp.bfloat16, jnp.float32
    dma = pltpu.SemaphoreType.DMA
    vmem = pltpu.VMEM
    summed = pl.pallas_call(
        kernel,
        out_shape=jax.ShapeDtypeStruct((8, WIDTH), f32),
        in_specs=[
            pl.BlockSpec(memory_space=pl.ANY),
            pl.BlockSpec(memory_space=pl.ANY),
            pl.BlockSpec(memory_space=pltpu.VMEM),
            pl.BlockSpec(memory_space=pl.ANY),
            pl.BlockSpec(memory_space=pltpu.VMEM),
        ],
        out_specs=pl.BlockSpec(memory_space=pltpu.VMEM),
        scratch_shapes=[
            vmem((WIDTH, UNITS), bf16),
            vmem((UNITS, WIDTH), bf16),
            vmem((CHUNKS, CHUNK, WIDTH), bf16),
            vmem((CHUNKS, CHUNK, UNITS), bf16),
            vmem((CHUNKS, 3, PIECE, UNITS), bf16),
            vmem((CHUNK, UNITS), f32),
            vmem((CHUNKS, PIECE, UNITS), bf16),
            vmem((CHUNKS, PIECE, UNITS), bf16),
            vmem((CHUNKS, CHUNK, UNITS), bf16),
            vmem((CHUNKS, CHUNK, WIDTH), f32),
            vmem((CHUNKS, 4, MINE, WIDTH), f32),
            vmem((CHUNKS, 3, MINE, WIDTH), bf16),
            vmem((CHUNKS, 3, MINE, WIDTH), bf16),
            vmem((CHUNKS, MINE, WIDTH), f32),
            vmem((8, 16, HALF), bf16),
            vmem((8, 16, HALF), bf16),
            dma((CHUNKS + 2,)),
            dma((CHUNKS, 3)), dma((CHUNKS, 3)),
            dma((CHUNKS, 4)), dma((CHUNKS, 4)),
            dma((CHUNKS, 3)), dma((CHUNKS, 3)),
            dma((CHUNKS,)), dma((CHUNKS,)),
            dma((CHUNKS, 3)), dma((CHUNKS, 3)),
            dma((CHUNKS, 4)), dma((CHUNKS, 4)),
            dma((CHUNKS, 3)), dma((CHUNKS, 3)),
            dma((8,)), dma((8,)),
        ],
        compiler_params=pltpu.CompilerParams(
            collective_id=0, has_side_effects=True, vmem_limit_bytes=40 * 2**20
        ),
        cost_estimate=pl.CostEstimate(
            flops=4 * TOKENS * WIDTH * UNITS, bytes_accessed=4 * WIDTH * UNITS, transcendentals=0
        ),
        name="feed_forward",
    )(tokens, weight_in, bias_in.reshape(1, UNITS), weight_out, bias_out.reshape(1, WIDTH))
    return summed.astype(jnp.bfloat16)


def solution(mesh):
    placed = (
        P("col", "row"),
        P("row", ("col", "depth")),
        P(("col", "depth")),
        P(("col", "depth"), "row"),
        P("row"),
    )
    return jax.shard_map(
        on_device, mesh=mesh, in_specs=placed, out_specs=P(("col", "depth"), "row"), check_vma=False
    )
```

time: 811 us -> 80.3 us (0.10)
  the two profiles are of different devices: /device:TPU:16 before, /device:TPU:480 now
where the time goes in v1:
time: 80.3 us; the launch traced here: 80 us
  Pallas kernels  73.7 us (92%)
  local copies, waits for them, and re-layouts  5.65 us (7%)
    pallas_call x1, Pallas kernels, on_device(): pl.pallas_call(kernel, out_shape=jax.ShapeDtypeStruct((8, WIDTH), f32), i...  73.7 us
    unnamed x6, local copies, waits for them, and re-layouts  4.26 us

profile of v1, /device:TPU:480, one launch (start us, length us, event | category | flops | bytes accessed | tf_op | source)
XLA Modules:
  0.0 80.0 jit_solution(16684896004252902405)
XLA Ops:
  0.0 0.7 reshape.6.bias_in
  0.7 0.7 reshape.7.bias_out
  1.4 0.0 copy-start
  1.4 1.7 %copy-done = bf16[1536,768]{1,0:T(8,128)(2,1)S(1)} copy-done((bf16[1536,768]{1,0:T(8,128)(2,1)S(1)}, bf16[1536,768]{1,0:T(8,128)(2,1)}, u32[]{:S(2)}) %copy-start) | copy-done | bytes 2359320
  3.1 0.0 copy-start.1
  3.1 1.7 %copy-done.1 = bf16[768,1536]{1,0:T(8,128)(2,1)S(1)} copy-done((bf16[768,1536]{1,0:T(8,128)(2,1)S(1)}, bf16[768,1536]{1,0:T(8,128)(2,1)}, u32[]{:S(2)}) %copy-start.1) | copy-done | bytes 2359320
  4.7 0.0 copy-start.2
  4.7 0.9 %copy-done.2 = bf16[64,1536]{1,0:T(8,128)(2,1)S(1)} copy-done((bf16[64,1536]{1,0:T(8,128)(2,1)S(1)}, bf16[64,1536]{1,0:T(8,128)(2,1)}, u32[]{:S(2)}) %copy-start.2) | copy-done | bytes 196632
  5.7 73.7 %feed_forward.1 = f32[8,1536]{1,0:T(8,128)S(1)} custom-call(bf16[64,1536]{1,0:T(8,128)(2,1)S(1)} %copy-done.2, bf16[1536,768]{1,0:T(8,128)(2,1)S(1)} %copy-done, f32[1,768]{1,0:T(1,128)S(1)} %reshape.6.bias_in, bf16[768,1536]{1,0:T(8,128)(2,1)S(1)} %copy-done.1, f32[1,1536]{1,0:T(1,128)S(1)} %reshape.7.bias_out), custom_call_target="tpu_custom_call" | custom-call | flops 2415919104 | bytes 4718592 | tf_op jit(solution)/shard_map/feed_forward/pallas_call | solution.py:253
  79.4 0.6 convert_element_type.3
Async XLA Ops:
  1.4 1.7 %copy-start = (bf16[1536,768]{1,0:T(8,128)(2,1)S(1)}, bf16[1536,768]{1,0:T(8,128)(2,1)}, u32[]{:S(2)}) copy-start(bf16[1536,768]{1,0:T(8,128)(2,1)} %weight_in.1) | copy-start | bytes 7077892
  3.1 1.7 %copy-start.1 = (bf16[768,1536]{1,0:T(8,128)(2,1)S(1)}, bf16[768,1536]{1,0:T(8,128)(2,1)}, u32[]{:S(2)}) copy-start(bf16[768,1536]{1,0:T(8,128)(2,1)} %weight_out.1) | copy-start | bytes 7077892
  4.7 0.9 %copy-start.2 = (bf16[64,1536]{1,0:T(8,128)(2,1)S(1)}, bf16[64,1536]{1,0:T(8,128)(2,1)}, u32[]{:S(2)}) copy-start(bf16[64,1536]{1,0:T(8,128)(2,1)} %tokens.1) | copy-start | bytes 589828

commit v2 on v0

v2 whole, which is shorter than its diff:
```python
import jax
import jax.numpy as jnp
from jax import lax
from jax.experimental import pallas as pl
from jax.experimental.pallas import tpu as pltpu
from jax.sharding import PartitionSpec as P

PARTS = ((0, None), (1, None), (2, None), (3, None))
N = len(PARTS)
TOKENS, WIDTH, UNITS = 512, 1536, 768
MINE = 16
SIDE = 4 * MINE
SIZES = [SIDE if e is not None else 2 * SIDE for _, e in PARTS]
BASES = [sum(SIZES[:k]) for k in range(N)]
PIECES = [size // 4 for size in SIZES]
TILE = 256
PACE = 1
HALF = WIDTH // 2


def schedule():
    order = []
    for t in range(N + 1):
        if t < N:
            order += [("gather", t), ("first_product", t)]
        if t >= 1:
            order += [("sum_pieces", t - 1)]
    for t in range(N + 3):
        for lag, stage in enumerate(("activate", "second_product", "sum_cores", "sum_x")):
            if 0 <= t - lag < N:
                order += [(stage, t - lag)]
    return order


def remote(src, dst, send, recv, device):
    return pltpu.make_async_remote_copy(
        src_ref=src,
        dst_ref=dst,
        send_sem=send,
        recv_sem=recv,
        device_id=device,
        device_id_type=pl.DeviceIdType.MESH,
    )


def kernel(
    tokens, weight_in, bias_in, weight_out, bias_out, out,
    w_in, w_out, b_in, b_out, gathered, pre_send, pre_recv, pre_sum, pre_out, pre_other, hidden,
    total, total_other, x_send, x_recv, x_sum, z_send, z_recv,
    local_sem, tok_ss, tok_rs, sib_ss, sib_rs, pre_ss, pre_rs, half_ss, half_rs,
    hid_ss, hid_rs, core_ss, core_rs, x_ss, x_rs, z_ss, z_rs, half_ready, depth_ready,
):
    row, col, depth = lax.axis_index("row"), lax.axis_index("col"), lax.axis_index("depth")
    y, z_hi, x, core = row // 2, row % 2, col // 2, col % 2

    def at_x(step):
        return {"col": ((x + step) % 4) * 2 + core}

    def at_y(step):
        return {"row": ((y + step) % 4) * 2 + z_hi}

    sibling = {"col": x * 2 + 1 - core}
    other_half = {"row": y * 2 + 1 - z_hi}

    def at_depth(d):
        return {"depth": d}

    def on_core(e, body):
        if e is None:
            body()
        else:
            pl.when(core == e)(body)

    def rows(start, size):
        return pl.ds(pl.multiple_of(start, 16), size)

    def core_rows(k, which):
        return rows(BASES[k] + (which * SIDE if PARTS[k][1] is None else 0), SIDE)

    def own_rows(k):
        return rows(BASES[k] + (core * SIDE if PARTS[k][1] is None else 0) + x * MINE, MINE)

    get_w_in = pltpu.make_async_copy(weight_in, w_in, local_sem.at[N])
    get_w_out = pltpu.make_async_copy(weight_out, w_out, local_sem.at[N + 1])
    get_b_in = pltpu.make_async_copy(bias_in, b_in.at[0], local_sem.at[N + 2])
    get_b_out = pltpu.make_async_copy(bias_out, b_out.at[0], local_sem.at[N + 3])
    get_own = [
        pltpu.make_async_copy(
            tokens.at[pl.ds(q * MINE, MINE)], gathered.at[own_rows(k)], local_sem.at[k]
        )
        for k, (q, _) in enumerate(PARTS)
    ]
    for k, (_, e) in enumerate(PARTS):
        on_core(e, get_own[k].start)
    get_w_in.start()
    get_b_in.start()

    def signal(semaphore, device):
        pl.semaphore_signal(
            semaphore, inc=1, device_id=device, device_id_type=pl.DeviceIdType.MESH
        )

    barrier = pltpu.get_barrier_semaphore()
    near = [at_x(1), at_x(2), at_x(3), at_y(1), at_y(2), at_y(3), sibling]
    for device in near:
        signal(barrier, device)

    @pl.when(z_hi == 0)
    def _():
        signal(barrier, other_half)

    for d in range(1, 8):
        @pl.when(depth < d)
        def _():
            signal(barrier, at_depth(d))

    pl.semaphore_wait(barrier, len(near) + z_hi + depth)

    def tok_copy(k, s):
        src = tokens.at[pl.ds(PARTS[k][0] * MINE, MINE)]
        return remote(src, gathered.at[own_rows(k)], tok_ss.at[k], tok_rs.at[k], at_x(s))

    def tok_all(k):
        place = gathered.at[pl.ds(BASES[k], 3 * MINE)]
        return remote(place, place, tok_ss.at[k], tok_rs.at[k], at_x(1))

    def sib_copy(k, which):
        place = gathered.at[core_rows(k, which)]
        return remote(place, place, sib_ss.at[k], sib_rs.at[k], sibling)

    def pre_slot(k, s):
        return pre_recv.at[pl.ds(BASES[k] // 4 * 3 + (s - 1) * PIECES[k], PIECES[k])]

    def pre_copy(k, s):
        piece = rows(BASES[k] + ((y + s) % 4) * PIECES[k], PIECES[k])
        return remote(pre_send.at[piece], pre_slot(k, s), pre_ss.at[k], pre_rs.at[k], at_y(s))

    def pre_all(k):
        place = pre_recv.at[pl.ds(BASES[k] // 4 * 3, 3 * PIECES[k])]
        return remote(place, place, pre_ss.at[k], pre_rs.at[k], at_y(1))

    def half_copy(k):
        piece = pl.ds(BASES[k] // 4, PIECES[k])
        return remote(
            pre_out.at[piece], pre_other.at[piece], half_ss.at[k], half_rs.at[k], other_half
        )

    def my_piece(k):
        return rows(BASES[k] + y * PIECES[k], PIECES[k])

    def hid_copy(k, s):
        place = hidden.at[my_piece(k)]
        return remote(place, place, hid_ss.at[k], hid_rs.at[k], at_y(s))

    def hid_all(k):
        place = hidden.at[pl.ds(BASES[k], 3 * PIECES[k])]
        return remote(place, place, hid_ss.at[k], hid_rs.at[k], at_y(1))

    def core_copy(k):
        return remote(
            total.at[core_rows(k, 1 - core)], total_other.at[k], core_ss.at[k], core_rs.at[k], sibling
        )

    def x_copy(k, s):
        return remote(x_send.at[k, s - 1], x_recv.at[k, s - 1], x_ss.at[k], x_rs.at[k], at_x(s))

    def x_all(k):
        return remote(x_send.at[k], x_recv.at[k], x_ss.at[k], x_rs.at[k], at_x(1))

    def z_copy(d, to):
        return remote(z_send.at[d], z_recv.at[depth], z_ss.at[d], z_rs, at_depth(to))

    def gather(k):
        e = PARTS[k][1]

        def body():
            get_own[k].wait()
            tok_all(k).wait_recv()
            sib_copy(k, core).start()

        on_core(e, body)

    def first_product(k):
        e = PARTS[k][1]
        on_core(None if e is None else 1 - e, lambda: sib_copy(k, 1 - core).wait_recv())
        if k == 0:
            get_w_in.wait()
            get_b_in.wait()
        part_rows = pl.ds(BASES[k], SIZES[k])

        def tile(i, _):
            units = pl.ds(pl.multiple_of(i * TILE, TILE), TILE)
            part = jnp.dot(
                gathered[part_rows, :], w_in[:, units], preferred_element_type=jnp.float32
            )
            pre_send[part_rows, units] = part.astype(jnp.bfloat16)
            pre_sum[part_rows, units] = part
            return 0

        lax.fori_loop(0, UNITS // TILE, tile, 0)
        for s in range(1, 4):
            pre_copy(k, s).start()

    def sum_pieces(k):
        acc = pre_sum[my_piece(k), :]
        pre_all(k).wait_recv()
        for s in range(1, 4):
            acc = acc + pre_slot(k, s)[...].astype(jnp.float32)
        pre_out[pl.ds(BASES[k] // 4, PIECES[k]), :] = acc.astype(jnp.bfloat16)
        if k == 0:
            @pl.when(z_hi == 0)
            def _():
                pl.semaphore_wait(half_ready, 1)

        if PACE and k >= PACE:
            half_copy(k - PACE).wait_send()
        half_copy(k).start()
        pre_sum[my_piece(k), :] = acc

    def activate(k):
        acc = pre_sum[my_piece(k), :] + b_in[...]
        half_copy(k).wait_recv()
        v = acc + pre_other[pl.ds(BASES[k] // 4, PIECES[k]), :].astype(jnp.float32)
        hidden[my_piece(k), :] = jax.nn.gelu(v, approximate=True).astype(jnp.bfloat16)
        for s in range(1, 4):
            hid_copy(k, s).start()

    def second_product(k):
        hid_all(k).wait_recv()
        if k == 0:
            get_w_out.wait()
            get_b_out.wait()
        part_rows = pl.ds(BASES[k], SIZES[k])

        def tile(i, _):
            cols = pl.ds(pl.multiple_of(i * TILE, TILE), TILE)
            total[part_rows, cols] = jnp.dot(
                hidden[part_rows, :], w_out[:, cols], preferred_element_type=jnp.float32
            )
            return 0

        lax.fori_loop(0, WIDTH // TILE, tile, 0)
        e = PARTS[k][1]
        on_core(None if e is None else 1 - e, lambda: core_copy(k).start())

    def sum_cores(k):
        e = PARTS[k][1]
        first = BASES[k] + (core * SIDE if e is None else 0)

        def body():
            core_copy(k).wait_recv()
            for s in (2, 1, 3, 0):
                i = (x + s) % 4
                part = total[rows(first + i * MINE, MINE), :] + total_other[k, rows(i * MINE, MINE), :]
                if s:
                    x_send[k, s - 1] = part.astype(jnp.bfloat16)
                    x_copy(k, s).start()
                else:
                    x_sum[k] = part

        on_core(e, body)

    def sum_x(k):
        q, e = PARTS[k]
        if k == 0:
            @pl.when(depth < 7)
            def _():
                pl.semaphore_wait(depth_ready, 7 - depth)

        def body():
            acc = x_sum[k]
            x_all(k).wait_recv()
            for s in range(1, 4):
                acc = acc + x_recv[k, s - 1].astype(jnp.float32)
            for n in range(2):
                d = 2 * q + n
                part = acc[n * 8:(n + 1) * 8]
                folded = jnp.concatenate([part[:, :HALF], part[:, HALF:]], axis=0)

                @pl.when(depth == d)
                def _():
                    out[...] = part

                @pl.when(depth != d)
                def _():
                    z_send[d] = folded.astype(jnp.bfloat16)
                    z_copy(d, d).start()

        on_core(e, body)

    def send_tokens(k):
        for s in (2, 1, 3):
            tok_copy(k, s).start()

    for k, (_, e) in enumerate(PARTS):
        on_core(e, lambda: send_tokens(k))

    @pl.when(z_hi == 1)
    def _():
        signal(half_ready, other_half)

    for d in range(7):
        @pl.when(depth > d)
        def _():
            signal(depth_ready, at_depth(d))

    get_w_out.start()
    get_b_out.start()

    stages = {
        f.__name__: f
        for f in (gather, first_product, sum_pieces, activate, second_product, sum_cores, sum_x)
    }
    for name, k in schedule():
        stages[name](k)

    for k, (_, e) in enumerate(PARTS):
        def sent():
            tok_all(k).wait_send()
            sib_copy(k, core).wait_send()
            x_all(k).wait_send()

        on_core(e, sent)
        on_core(None if e is None else 1 - e, lambda: core_copy(k).wait_send())
        pre_all(k).wait_send()
        hid_all(k).wait_send()
        if not PACE or k >= N - PACE:
            half_copy(k).wait_send()
    for d in range(8):
        @pl.when(depth != d)
        def _():
            z_copy(d, d).wait_send()

    acc = out[...] + b_out[...]
    seven = z_recv.at[pl.ds(0, 7)]
    remote(seven, seven, z_ss.at[0], z_rs, at_depth(depth)).wait_recv()
    for s in range(1, 8):
        part = z_recv[(depth + s) % 8].astype(jnp.float32)
        acc = acc + jnp.concatenate([part[:8], part[8:]], axis=1)
    out[...] = acc


def on_device(tokens, weight_in, bias_in, weight_out, bias_out):
    bf16, f32 = jnp.bfloat16, jnp.float32
    dma = pltpu.SemaphoreType.DMA
    vmem = pltpu.VMEM
    summed = pl.pallas_call(
        kernel,
        out_shape=jax.ShapeDtypeStruct((8, WIDTH), f32),
        in_specs=[
            pl.BlockSpec(memory_space=pltpu.HBM),
            pl.BlockSpec(memory_space=pltpu.HBM),
            pl.BlockSpec(memory_space=pltpu.HBM),
            pl.BlockSpec(memory_space=pltpu.HBM),
            pl.BlockSpec(memory_space=pltpu.HBM),
        ],
        out_specs=pl.BlockSpec(memory_space=pltpu.VMEM),
        scratch_shapes=[
            vmem((WIDTH, UNITS), bf16),
            vmem((UNITS, WIDTH), bf16),
            vmem((1, UNITS), f32),
            vmem((1, WIDTH), f32),
            vmem((TOKENS, WIDTH), bf16),
            vmem((TOKENS, UNITS), bf16),
            vmem((TOKENS // 4 * 3, UNITS), bf16),
            vmem((TOKENS, UNITS), f32),
            vmem((TOKENS // 4, UNITS), bf16),
            vmem((TOKENS // 4, UNITS), bf16),
            vmem((TOKENS, UNITS), bf16),
            vmem((TOKENS, WIDTH), f32),
            vmem((N, SIDE, WIDTH), f32),
            vmem((N, 3, MINE, WIDTH), bf16),
            vmem((N, 3, MINE, WIDTH), bf16),
            vmem((N, MINE, WIDTH), f32),
            vmem((8, 16, HALF), bf16),
            vmem((8, 16, HALF), bf16),
            dma((N + 4,)),
            dma((N,)), dma((N,)),
            dma((N,)), dma((N,)),
            dma((N,)), dma((N,)),
            dma((N,)), dma((N,)),
            dma((N,)), dma((N,)),
            dma((N,)), dma((N,)),
            dma((N,)), dma((N,)),
            dma((8,)), dma,
            pltpu.SemaphoreType.REGULAR, pltpu.SemaphoreType.REGULAR,
        ],
        compiler_params=pltpu.CompilerParams(
            collective_id=0, has_side_effects=True, vmem_limit_bytes=60 * 2**20
        ),
        cost_estimate=pl.CostEstimate(
            flops=4 * TOKENS * WIDTH * UNITS, bytes_accessed=4 * WIDTH * UNITS, transcendentals=0
        ),
        name="feed_forward",
    )(tokens, weight_in, bias_in, weight_out, bias_out)
    return summed.astype(jnp.bfloat16)


def solution(mesh):
    placed = (
        P("col", "row"),
        P("row", ("col", "depth")),
        P(("col", "depth")),
        P(("col", "depth"), "row"),
        P("row"),
    )
    return jax.shard_map(
        on_device, mesh=mesh, in_specs=placed, out_specs=P(("col", "depth"), "row"), check_vma=False
    )
```

time: 811 us -> 66.7 us (0.08)
  the two profiles are of different devices: /device:TPU:16 before, /device:TPU:32 now
where the time goes in v2:
time: 66.7 us; the launch traced here: 66.6 us
  Pallas kernels  65.1 us (98%)
  other arithmetic  1.41 us (2%)
    pallas_call x1, Pallas kernels, on_device(): pl.pallas_call(kernel, out_shape=jax.ShapeDtypeStruct((8, WIDTH), f32), i...  65.1 us
    convert_element_type x1, other arithmetic, on_device(): return summed.astype(jnp.bfloat16)  1.41 us

profile of v2, /device:TPU:32, one launch (start us, length us, event | category | flops | bytes accessed | tf_op | source)
XLA Modules:
  0.0 66.6 jit_solution(3994900696441504193)
XLA Ops:
  0.0 65.1 %feed_forward.1 = f32[8,1536]{1,0:T(8,128)} custom-call(bf16[64,1536]{1,0:T(8,128)(2,1)} %tokens.1, bf16[1536,768]{1,0:T(8,128)(2,1)} %weight_in.1, f32[768]{0:T(1024)} %bias_in.1, bf16[768,1536]{1,0:T(8,128)(2,1)} %weight_out.1, f32[1536]{0:T(1024)} %bias_out.1), custom_call_target="tpu_custom_call" | custom-call | flops 2415919104 | bytes 4718592 | tf_op jit(solution)/shard_map/feed_forward/pallas_call | solution.py:347
  65.2 1.4 %convert_element_type.3 = bf16[8,1536]{1,0:T(8,128)(2,1)} convert(f32[8,1536]{1,0:T(8,128)} %feed_forward.1) | non-fusion elementwise | flops 12288 | bytes 73728 | tf_op jit(solution)/shard_map/convert_element_type | solution.py:396

commit v3 on v2

--- a/solution.py
+++ b/solution.py
@@ -5,7 +5,7 @@
 from jax.experimental.pallas import tpu as pltpu
 from jax.sharding import PartitionSpec as P
 
-PARTS = ((0, None), (1, None), (2, None), (3, None))
+PARTS = tuple((q, e) for q in (0, 1, 3, 2) for e in (1, 0))
 N = len(PARTS)
 TOKENS, WIDTH, UNITS = 512, 1536, 768
 MINE = 16
@@ -14,21 +14,16 @@
 BASES = [sum(SIZES[:k]) for k in range(N)]
 PIECES = [size // 4 for size in SIZES]
 TILE = 256
-PACE = 1
 HALF = WIDTH // 2
 
 
 def schedule():
+    before = {"gather": 0, "first_product": 0, "sum_pieces": 2}
+    after = {"activate": 0, "second_product": 2, "sum_cores": 3, "sum_x": 5}
     order = []
-    for t in range(N + 1):
-        if t < N:
-            order += [("gather", t), ("first_product", t)]
-        if t >= 1:
-            order += [("sum_pieces", t - 1)]
-    for t in range(N + 3):
-        for lag, stage in enumerate(("activate", "second_product", "sum_cores", "sum_x")):
-            if 0 <= t - lag < N:
-                order += [(stage, t - lag)]
+    for lags in (before, after):
+        steps = [(k + lag, n, k) for n, lag in enumerate(lags.values()) for k in range(N)]
+        order += [(list(lags)[n], k) for _, n, k in sorted(steps)]
     return order
 
 
@@ -212,8 +207,6 @@
             def _():
                 pl.semaphore_wait(half_ready, 1)
 
-        if PACE and k >= PACE:
-            half_copy(k - PACE).wait_send()
         half_copy(k).start()
         pre_sum[my_piece(k), :] = acc
 
@@ -324,8 +317,7 @@
         on_core(None if e is None else 1 - e, lambda: core_copy(k).wait_send())
         pre_all(k).wait_send()
         hid_all(k).wait_send()
-        if not PACE or k >= N - PACE:
-            half_copy(k).wait_send()
+        half_copy(k).wait_send()
     for d in range(8):
         @pl.when(depth != d)
         def _():

time: 66.7 us -> 62.5 us (0.937)
  the two profiles are of different devices: /device:TPU:32 before, /device:TPU:128 now
where the time goes in v3:
time: 62.5 us; the launch traced here: 62.4 us
  Pallas kernels  61 us (98%)
  other arithmetic  1.41 us (2%)
    pallas_call x1, Pallas kernels, on_device(): pl.pallas_call(kernel, out_shape=jax.ShapeDtypeStruct((8, WIDTH), f32), i...  61 us
    convert_element_type x1, other arithmetic, on_device(): return summed.astype(jnp.bfloat16)  1.41 us

profile of v3, /device:TPU:128, one launch (start us, length us, event | category | flops | bytes accessed | tf_op | source)
XLA Modules:
  0.0 62.4 jit_solution(15370414056911698584)
XLA Ops:
  0.0 61.0 %feed_forward.1 = f32[8,1536]{1,0:T(8,128)} custom-call(bf16[64,1536]{1,0:T(8,128)(2,1)} %tokens.1, bf16[1536,768]{1,0:T(8,128)(2,1)} %weight_in.1, f32[768]{0:T(1024)} %bias_in.1, bf16[768,1536]{1,0:T(8,128)(2,1)} %weight_out.1, f32[1536]{0:T(1024)} %bias_out.1), custom_call_target="tpu_custom_call" | custom-call | flops 2415919104 | bytes 4718592 | tf_op jit(solution)/shard_map/feed_forward/pallas_call | solution.py:339
  61.0 1.4 %convert_element_type.3 = bf16[8,1536]{1,0:T(8,128)(2,1)} convert(f32[8,1536]{1,0:T(8,128)} %feed_forward.1) | non-fusion elementwise | flops 12288 | bytes 73728 | tf_op jit(solution)/shard_map/convert_element_type | solution.py:388

commit v4 on v3

--- a/solution.py
+++ b/solution.py
@@ -14,16 +14,17 @@
 BASES = [sum(SIZES[:k]) for k in range(N)]
 PIECES = [size // 4 for size in SIZES]
 TILE = 256
+AHEAD = 3
 HALF = WIDTH // 2
 
 
 def schedule():
-    before = {"gather": 0, "first_product": 0, "sum_pieces": 2}
-    after = {"activate": 0, "second_product": 2, "sum_cores": 3, "sum_x": 5}
-    order = []
-    for lags in (before, after):
-        steps = [(k + lag, n, k) for n, lag in enumerate(lags.values()) for k in range(N)]
-        order += [(list(lags)[n], k) for _, n, k in sorted(steps)]
+    lags = {
+        "gather": 0, "first_product": 0, "sum_pieces": 2,
+        "activate": 7, "second_product": 9, "sum_cores": 10, "sum_x": 12,
+    }
+    steps = sorted((k + lag, n, k) for n, lag in enumerate(lags.values()) for k in range(N))
+    order = [(list(lags)[n], k) for _, n, k in steps]
     return order
 
 
@@ -165,6 +166,10 @@
     def z_copy(d, to):
         return remote(z_send.at[d], z_recv.at[depth], z_ss.at[d], z_rs, at_depth(to))
 
+    def send_tokens(k):
+        for s in (2, 1, 3):
+            tok_copy(k, s).start()
+
     def gather(k):
         e = PARTS[k][1]
 
@@ -174,6 +179,8 @@
             sib_copy(k, core).start()
 
         on_core(e, body)
+        if k + AHEAD < N:
+            on_core(PARTS[k + AHEAD][1], lambda: send_tokens(k + AHEAD))
 
     def first_product(k):
         e = PARTS[k][1]
@@ -281,12 +288,8 @@
 
         on_core(e, body)
 
-    def send_tokens(k):
-        for s in (2, 1, 3):
-            tok_copy(k, s).start()
-
-    for k, (_, e) in enumerate(PARTS):
-        on_core(e, lambda: send_tokens(k))
+    for k in range(AHEAD):
+        on_core(PARTS[k][1], lambda: send_tokens(k))
 
     @pl.when(z_hi == 1)
     def _():

time: 62.5 us -> 62.4 us (level)
  no operation moved by 1% of the time
where the time goes in v4:
time: 62.4 us; the launch traced here: 62.3 us
  Pallas kernels  60.8 us (97%)
  other arithmetic  1.41 us (2%)
    pallas_call x1, Pallas kernels, on_device(): pl.pallas_call(kernel, out_shape=jax.ShapeDtypeStruct((8, WIDTH), f32), i...  60.8 us
    convert_element_type x1, other arithmetic, on_device(): return summed.astype(jnp.bfloat16)  1.41 us

profile of v4, /device:TPU:128, one launch (start us, length us, event | category | flops | bytes accessed | tf_op | source)
XLA Modules:
  0.0 62.3 jit_solution(10228548855870166205)
XLA Ops:
  0.0 60.8 %feed_forward.1 = f32[8,1536]{1,0:T(8,128)} custom-call(bf16[64,1536]{1,0:T(8,128)(2,1)} %tokens.1, bf16[1536,768]{1,0:T(8,128)(2,1)} %weight_in.1, f32[768]{0:T(1024)} %bias_in.1, bf16[768,1536]{1,0:T(8,128)(2,1)} %weight_out.1, f32[1536]{0:T(1024)} %bias_out.1), custom_call_target="tpu_custom_call" | custom-call | flops 2415919104 | bytes 4718592 | tf_op jit(solution)/shard_map/feed_forward/pallas_call | solution.py:342
  60.8 1.4 %convert_element_type.3 = bf16[8,1536]{1,0:T(8,128)(2,1)} convert(f32[8,1536]{1,0:T(8,128)} %feed_forward.1) | non-fusion elementwise | flops 12288 | bytes 73728 | tf_op jit(solution)/shard_map/convert_element_type | solution.py:391
